TPU v7x, 32 devices: a whole 2x2x4 slice. The times are simulated.
32 devices in a mesh: groups: 2 (over x), ctx: 8 (over z, y), heads: 2 (over core).
Axes of the slice: x: 2, y: 2, z: 4, core: 2. Of those that a mesh axis runs over, the one named last changes fastest.
Arguments:
- query_vectors: bfloat16 [2048, 16, 128], P(('groups', 'ctx'), 'heads'), parts along dimension 0, may hold values from -5.5 to 5.5
- key_vectors: bfloat16 [2048, 4, 128], P(('groups', 'ctx'), 'heads'), parts along dimension 0, may hold values from -5.5 to 5.5
- value_rows: bfloat16 [2048, 4, 128], P(('groups', 'ctx'), 'heads'), parts along dimension 0, may hold values from -6 to 6
- forward_out: bfloat16 [2048, 16, 128], P(('groups', 'ctx'), 'heads'), parts along dimension 0, may hold values from -3 to 3
- out_grad: bfloat16 [2048, 16, 128], P(('groups', 'ctx'), 'heads'), parts along dimension 0, may hold values from -24 to 24
- block_offsets: int32 [16], P(('groups', 'ctx')), parts along dimension 0, may hold values from 0 to 7, each once
Outputs:
- query_grad: float32 [2048, 16, 128], P(('groups', 'ctx'), 'heads'), parts along dimension 0
- key_gradient_array: float32 [2048, 4, 128], P(('groups', 'ctx'), 'heads'), parts along dimension 0
- value_gradient_array: float32 [2048, 4, 128], P(('groups', 'ctx'), 'heads'), parts along dimension 0
There are 2 independent parts, one for each index of `groups`. A program takes and returns all parts, laid end to end along the dimension named above; each array names one. Nothing has to cross between parts.
Inputs may be any that keep to these rules, and one draw needn't show every extreme that they name: block_offsets is a permutation of 0 to 7.
All inputs are finite; a program needn't handle non-finite values.
Results may differ from a plain program's by a relative error of at most 0.0029.
Values may be sent and summed in bfloat16 or wider, within the bound.
A program may use at most 64 MiB of HBM per device.

v0:
```python
import jax
import jax.numpy as jnp
from jax import lax
from jax.sharding import PartitionSpec as P


def passed_along(value, axis, by):
    peers = lax.axis_size(axis)
    return lax.ppermute(value, axis, [(i, (i + by) % peers) for i in range(peers)])


def on_device(query_vectors, key_vectors, value_rows, forward_out, out_grad, block_offsets):
    tok_rows, q_heads, head_width = query_vectors.shape
    kv_heads = key_vectors.shape[1]
    heads_per_group = q_heads // kv_heads
    cycle_size = lax.axis_size("ctx")
    cycle_index = lax.axis_index("ctx")
    block_starts = lax.all_gather(block_offsets, "ctx", axis=0, tiled=True)
    score_scale = head_width ** (-0.5)
    row_index = jnp.arange(tok_rows, dtype=jnp.int32)
    own_positions = block_offsets[0] * tok_rows + row_index
    grouped_query = query_vectors.reshape(tok_rows, kv_heads, heads_per_group, head_width)
    grouped_grad = out_grad.reshape(tok_rows, kv_heads, heads_per_group, head_width)
    row_delta = jnp.sum(out_grad.astype(jnp.float32) * forward_out.astype(jnp.float32), axis=2)
    row_delta = row_delta.reshape(tok_rows, kv_heads, heads_per_group).transpose(1, 2, 0)

    def masked_scores(key_block, source_block):
        key_positions = block_starts[source_block] * tok_rows + row_index
        visible = key_positions[None, :] <= own_positions[:, None]
        scores = (
            jnp.einsum(
                "ighd,jgd->ghij", grouped_query, key_block, preferred_element_type=jnp.float32
            )
            * score_scale
        )
        return (jnp.where(visible, scores, -1e30), visible)

    def stats_update(running, key_block, source_block):
        run_max, run_total = running
        scores, visible = masked_scores(key_block, source_block)
        new_max = jnp.maximum(run_max, jnp.max(scores, axis=3))
        new_total = run_total * jnp.exp(run_max - new_max) + jnp.sum(
            jnp.exp(scores - new_max[..., None]), axis=3
        )
        return (new_max, new_total)

    def stats_step(running, key_block, source_block):
        return stats_update(running, key_block, source_block)

    head_shape = (kv_heads, heads_per_group, tok_rows)
    running = (jnp.full(head_shape, -1e30, jnp.float32), jnp.zeros(head_shape, jnp.float32))
    pair_shape = (2, tok_rows, kv_heads, head_width)
    zero_pair = jnp.zeros(pair_shape, jnp.float32)
    query_grad = jnp.zeros((tok_rows, kv_heads, heads_per_group, head_width), jnp.float32)

    def grad_update(grad_state, key_block, value_block, source_block, log_total):
        query_grad, grad_pair = grad_state
        scores, visible = masked_scores(key_block, source_block)
        probs = jnp.where(visible, jnp.exp(scores - log_total[..., None]), 0.0)
        probs_low = probs.astype(jnp.bfloat16)
        prob_grad = jnp.einsum(
            "ighd,jgd->ghij", grouped_grad, value_block, preferred_element_type=jnp.float32
        )
        score_grad = (probs * (prob_grad - row_delta[..., None])).astype(jnp.bfloat16)
        query_grad = query_grad + score_scale * jnp.einsum(
            "ghij,jgd->ighd", score_grad, key_block, preferred_element_type=jnp.float32
        )
        key_part = score_scale * jnp.einsum(
            "ghij,ighd->jgd", score_grad, grouped_query, preferred_element_type=jnp.float32
        )
        value_part = jnp.einsum(
            "ghij,ighd->jgd", probs_low, grouped_grad, preferred_element_type=jnp.float32
        )
        return (query_grad, grad_pair + jnp.stack([key_part, value_part]))

    def grad_step(grad_state, key_block, value_block, source_block, log_total):
        return grad_update(grad_state, key_block, value_block, source_block, log_total)

    running = stats_step(running, key_vectors, cycle_index)

    def stats_loop(cycle_step, loop_carry):
        running, key_block = loop_carry
        key_block = passed_along(key_block, "ctx", 1)
        source_block = (cycle_index - cycle_step) % cycle_size
        running = stats_step(running, key_block, source_block)
        return (running, key_block)

    running, unused_block = lax.fori_loop(1, cycle_size, stats_loop, (running, key_vectors))
    log_total = running[0] + jnp.log(running[1])
    travelling = jnp.stack([key_vectors, value_rows])
    grad_pair = zero_pair

    def cycle_update(query_grad, grad_pair, travelling, source_block):
        key_block, value_block = (travelling[0], travelling[1])
        return grad_step((query_grad, grad_pair), key_block, value_block, source_block, log_total)

    query_grad, grad_pair = cycle_update(query_grad, grad_pair, travelling, cycle_index)

    def back_loop(cycle_step, loop_carry):
        query_grad, grad_pair, travelling = loop_carry
        travelling = passed_along(travelling, "ctx", 1)
        grad_pair = passed_along(grad_pair, "ctx", 1)
        source_block = (cycle_index - cycle_step) % cycle_size
        query_grad, grad_pair = cycle_update(query_grad, grad_pair, travelling, source_block)
        return (query_grad, grad_pair, travelling)

    query_grad, grad_pair, travelling = lax.fori_loop(
        1, cycle_size, back_loop, (query_grad, grad_pair, travelling)
    )
    grad_pair = passed_along(grad_pair, "ctx", 1)
    return (query_grad.reshape(tok_rows, q_heads, head_width), grad_pair[0], grad_pair[1])


def solution(mesh):
    in_specs = (
        P(("groups", "ctx"), "heads", None),
        P(("groups", "ctx"), "heads", None),
        P(("groups", "ctx"), "heads", None),
        P(("groups", "ctx"), "heads", None),
        P(("groups", "ctx"), "heads", None),
        P(("groups", "ctx")),
    )
    out_specs = (
        P(("groups", "ctx"), "heads", None),
        P(("groups", "ctx"), "heads", None),
        P(("groups", "ctx"), "heads", None),
    )
    return jax.shard_map(
        on_device, mesh=mesh, in_specs=in_specs, out_specs=out_specs, check_vma=False
    )
```

profile of v0, /device:TPU:0, one launch (start us, length us, event | category | flops | bytes accessed | tf_op | source)
XLA Modules:
  0.0 167.6 jit_solution(2116778922920582532)
XLA Ops:
  1.4 0.6 dynamic-slice
  1.9 0.8 dynamic-update-slice
  2.7 13.1 %all-reduce = s32[8]{0:T(128)S(1)} all-reduce(s32[8]{0:T(128)S(1)} %dynamic-update-slice), channel_id=1, replica_groups=mesh['groups'=2,'ctx'=8,'heads'=2] {'ctx'}, use_global_device_ids=true, to_apply=%add | all-reduce | flops 8 | bytes 64
  15.8 0.6 dynamic_slice.24
  17.0 0.9 copy.77
  17.9 0.6 copy-done.1
  18.5 0.9 copy-done.6
  19.7 0.8 copy-done.5
  20.7 0.7 copy-done.4
  21.8 0.7 copy-done.3
  22.5 53.4 %while.40 = (s32[]{:T(128)}, f32[2,4,128]{2,1,0:T(4,128)S(1)}, f32[2,4,128]{2,1,0:T(4,128)S(1)}, bf16[128,2,128]{2,0,1:T(8,128)(2,1)S(1)}, s32[]{:T(128)}, /*ind...) while((s32[]{:T(128)}, f32[2,4,128]{2,1,0:T(4,128)S(1)}, ...), condition=%wide.region_5.6_spmd.clone, body=%wide.region_2.5_spmd.clone.sunk | while | flops 34228496 | bytes 1857888 | solution.py:88
  22.5 1.5 collective-permute-start
  24.0 0.6 dynamic_slice.29
  25.3 4.1 %collective-permute-done = bf16[128,2,128]{2,0,1:T(8,128)(2,1)S(1)} collective-permute-done((bf16[128,2,128]{2,0,1:T(8,128)(2,1)S(1)}, bf16[128,2,128]{2,0,1:T(8,128)(2,1)S(1)}, u32[]{:S(2)}, u32[]{:S(2)}) %collective-permute-start) | collective-permute-done | bytes 65568 | tf_op jit(solution)/shard_map/while/body/eval_jaxpr/ppermute | solution.py:9
  29.9 0.6 dynamic_slice.29
  31.3 5.6 %collective-permute-done = bf16[128,2,128]{2,0,1:T(8,128)(2,1)S(1)} collective-permute-done((bf16[128,2,128]{2,0,1:T(8,128)(2,1)S(1)}, bf16[128,2,128]{2,0,1:T(8,128)(2,1)S(1)}, u32[]{:S(2)}, u32[]{:S(2)}) %collective-permute-start) | collective-permute-done | bytes 65568 | tf_op jit(solution)/shard_map/while/body/eval_jaxpr/ppermute | solution.py:9
  37.4 0.6 dynamic_slice.29
  38.7 6.3 %collective-permute-done = bf16[128,2,128]{2,0,1:T(8,128)(2,1)S(1)} collective-permute-done((bf16[128,2,128]{2,0,1:T(8,128)(2,1)S(1)}, bf16[128,2,128]{2,0,1:T(8,128)(2,1)S(1)}, u32[]{:S(2)}, u32[]{:S(2)}) %collective-permute-start) | collective-permute-done | bytes 65568 | tf_op jit(solution)/shard_map/while/body/eval_jaxpr/ppermute | solution.py:9
  45.4 0.6 dynamic_slice.29
  46.8 5.6 %collective-permute-done = bf16[128,2,128]{2,0,1:T(8,128)(2,1)S(1)} collective-permute-done((bf16[128,2,128]{2,0,1:T(8,128)(2,1)S(1)}, bf16[128,2,128]{2,0,1:T(8,128)(2,1)S(1)}, u32[]{:S(2)}, u32[]{:S(2)}) %collective-permute-start) | collective-permute-done | bytes 65568 | tf_op jit(solution)/shard_map/while/body/eval_jaxpr/ppermute | solution.py:9
  52.9 0.6 dynamic_slice.29
  54.2 5.6 %collective-permute-done = bf16[128,2,128]{2,0,1:T(8,128)(2,1)S(1)} collective-permute-done((bf16[128,2,128]{2,0,1:T(8,128)(2,1)S(1)}, bf16[128,2,128]{2,0,1:T(8,128)(2,1)S(1)}, u32[]{:S(2)}, u32[]{:S(2)}) %collective-permute-start) | collective-permute-done | bytes 65568 | tf_op jit(solution)/shard_map/while/body/eval_jaxpr/ppermute | solution.py:9
  60.3 0.6 dynamic_slice.29
  61.6 5.6 %collective-permute-done = bf16[128,2,128]{2,0,1:T(8,128)(2,1)S(1)} collective-permute-done((bf16[128,2,128]{2,0,1:T(8,128)(2,1)S(1)}, bf16[128,2,128]{2,0,1:T(8,128)(2,1)S(1)}, u32[]{:S(2)}, u32[]{:S(2)}) %collective-permute-start) | collective-permute-done | bytes 65568 | tf_op jit(solution)/shard_map/while/body/eval_jaxpr/ppermute | solution.py:9
  67.7 0.6 dynamic_slice.29
  69.1 6.4 %collective-permute-done = bf16[128,2,128]{2,0,1:T(8,128)(2,1)S(1)} collective-permute-done((bf16[128,2,128]{2,0,1:T(8,128)(2,1)S(1)}, bf16[128,2,128]{2,0,1:T(8,128)(2,1)S(1)}, u32[]{:S(2)}, u32[]{:S(2)}) %collective-permute-start) | collective-permute-done | bytes 65568 | tf_op jit(solution)/shard_map/while/body/eval_jaxpr/ppermute | solution.py:9
  76.6 0.3 fusion.26
  76.8 0.5 copy-done.2
  77.4 80.1 %while.41 = (s32[]{:T(128)}, f32[128,2,4,128]{3,0,2,1:T(8,128)S(1)}, f32[2,128,2,128]{3,1,2,0:T(8,128)S(1)}, bf16[2,128,2,128]{3,1,2,0:T(8,128)(2,1)S(1)}, s32[]...) while((s32[]{:T(128)}, ...), condition=%wide.region_8.9_spmd.clone, body=%wide.region_7.8_spmd.clone.sunk | while | flops 169263376 | bytes 7580064 | solution.py:107
  77.6 0.6 dynamic_slice.30
  79.0 7.7 %collective-permute-done.1 = bf16[2,128,2,128]{3,1,2,0:T(8,128)(2,1)S(1)} collective-permute-done((bf16[2,128,2,128]{3,1,2,0:T(8,128)(2,1)S(1)}, bf16[2,128,2,128]{3,1,2,0:T(8,128)(2,1)S(1)}, u32[]{:S(2)}, u32[]{:S(2)}) %collective-permute-start.1) | collective-permute-done | bytes 131104 | tf_op jit(solution)/shard_map/while/body/eval_jaxpr/ppermute | solution.py:9
  86.6 0.3 fusion.78
  87.6 0.3 fusion.80
  87.9 1.8 %collective-permute-done.2 = f32[2,128,2,128]{3,1,2,0:T(8,128)S(1)} collective-permute-done((f32[2,128,2,128]{3,1,2,0:T(8,128)S(1)}, f32[2,128,2,128]{3,1,2,0:T(8,128)S(1)}, u32[]{:S(2)}, u32[]{:S(2)}) %collective-permute-start.2) | collective-permute-done | bytes 262176 | tf_op jit(solution)/shard_map/while/body/eval_jaxpr/ppermute | solution.py:9
  90.0 0.6 dynamic_slice.30
  91.3 7.1 %collective-permute-done.1 = bf16[2,128,2,128]{3,1,2,0:T(8,128)(2,1)S(1)} collective-permute-done((bf16[2,128,2,128]{3,1,2,0:T(8,128)(2,1)S(1)}, bf16[2,128,2,128]{3,1,2,0:T(8,128)(2,1)S(1)}, u32[]{:S(2)}, u32[]{:S(2)}) %collective-permute-start.1) | collective-permute-done | bytes 131104 | tf_op jit(solution)/shard_map/while/body/eval_jaxpr/ppermute | solution.py:9
  98.4 0.3 fusion.78
  99.4 0.3 fusion.80
  99.7 1.5 collective-permute-done.2
  101.4 0.6 dynamic_slice.30
  102.8 6.2 %collective-permute-done.1 = bf16[2,128,2,128]{3,1,2,0:T(8,128)(2,1)S(1)} collective-permute-done((bf16[2,128,2,128]{3,1,2,0:T(8,128)(2,1)S(1)}, bf16[2,128,2,128]{3,1,2,0:T(8,128)(2,1)S(1)}, u32[]{:S(2)}, u32[]{:S(2)}) %collective-permute-start.1) | collective-permute-done | bytes 131104 | tf_op jit(solution)/shard_map/while/body/eval_jaxpr/ppermute | solution.py:9
  110.0 0.3 fusion.80
  110.3 1.5 collective-permute-done.2
  112.0 0.6 dynamic_slice.30
  113.3 6.2 %collective-permute-done.1 = bf16[2,128,2,128]{3,1,2,0:T(8,128)(2,1)S(1)} collective-permute-done((bf16[2,128,2,128]{3,1,2,0:T(8,128)(2,1)S(1)}, bf16[2,128,2,128]{3,1,2,0:T(8,128)(2,1)S(1)}, u32[]{:S(2)}, u32[]{:S(2)}) %collective-permute-start.1) | collective-permute-done | bytes 131104 | tf_op jit(solution)/shard_map/while/body/eval_jaxpr/ppermute | solution.py:9
  119.6 0.3 fusion.78
  120.6 0.3 fusion.80
  120.9 1.6 collective-permute-done.2
  122.7 0.6 dynamic_slice.30
  124.1 6.2 %collective-permute-done.1 = bf16[2,128,2,128]{3,1,2,0:T(8,128)(2,1)S(1)} collective-permute-done((bf16[2,128,2,128]{3,1,2,0:T(8,128)(2,1)S(1)}, bf16[2,128,2,128]{3,1,2,0:T(8,128)(2,1)S(1)}, u32[]{:S(2)}, u32[]{:S(2)}) %collective-permute-start.1) | collective-permute-done | bytes 131104 | tf_op jit(solution)/shard_map/while/body/eval_jaxpr/ppermute | solution.py:9
  131.3 0.3 fusion.80
  131.6 2.7 %collective-permute-done.2 = f32[2,128,2,128]{3,1,2,0:T(8,128)S(1)} collective-permute-done((f32[2,128,2,128]{3,1,2,0:T(8,128)S(1)}, f32[2,128,2,128]{3,1,2,0:T(8,128)S(1)}, u32[]{:S(2)}, u32[]{:S(2)}) %collective-permute-start.2) | collective-permute-done | bytes 262176 | tf_op jit(solution)/shard_map/while/body/eval_jaxpr/ppermute | solution.py:9
  134.5 0.6 dynamic_slice.30
  135.8 6.2 %collective-permute-done.1 = bf16[2,128,2,128]{3,1,2,0:T(8,128)(2,1)S(1)} collective-permute-done((bf16[2,128,2,128]{3,1,2,0:T(8,128)(2,1)S(1)}, bf16[2,128,2,128]{3,1,2,0:T(8,128)(2,1)S(1)}, u32[]{:S(2)}, u32[]{:S(2)}) %collective-permute-start.1) | collective-permute-done | bytes 131104 | tf_op jit(solution)/shard_map/while/body/eval_jaxpr/ppermute | solution.py:9
  142.0 0.3 fusion.78
  143.0 0.3 fusion.80
  143.4 3.6 %collective-permute-done.2 = f32[2,128,2,128]{3,1,2,0:T(8,128)S(1)} collective-permute-done((f32[2,128,2,128]{3,1,2,0:T(8,128)S(1)}, f32[2,128,2,128]{3,1,2,0:T(8,128)S(1)}, u32[]{:S(2)}, u32[]{:S(2)}) %collective-permute-start.2) | collective-permute-done | bytes 262176 | tf_op jit(solution)/shard_map/while/body/eval_jaxpr/ppermute | solution.py:9
  147.1 0.6 dynamic_slice.30
  148.5 6.2 %collective-permute-done.1 = bf16[2,128,2,128]{3,1,2,0:T(8,128)(2,1)S(1)} collective-permute-done((bf16[2,128,2,128]{3,1,2,0:T(8,128)(2,1)S(1)}, bf16[2,128,2,128]{3,1,2,0:T(8,128)(2,1)S(1)}, u32[]{:S(2)}, u32[]{:S(2)}) %collective-permute-start.1) | collective-permute-done | bytes 131104 | tf_op jit(solution)/shard_map/while/body/eval_jaxpr/ppermute | solution.py:9
  155.7 0.3 fusion.80
  156.0 1.5 collective-permute-done.2
  157.8 1.1 copy.45
  159.0 7.9 %collective-permute-done.3 = f32[2,128,2,128]{3,2,1,0:T(2,128)S(1)} collective-permute-done((f32[2,128,2,128]{3,2,1,0:T(2,128)S(1)}, f32[2,128,2,128]{3,2,1,0:T(2,128)S(1)}, u32[]{:S(2)}, u32[]{:S(2)}) %collective-permute-start.3) | collective-permute-done | bytes 262176 | tf_op jit(solution)/shard_map/ppermute | solution.py:9
  166.9 0.7 slice_bitcast_fusion.5
  (167 shorter events, 12.6 us)
Async XLA Ops:
  0.6 0.7 copy-start.8
  0.6 17.8 %copy-start = (bf16[128,8,128]{2,1,0:T(8,128)(2,1)S(1)}, bf16[128,8,128]{2,1,0:T(8,128)(2,1)}, u32[]{:S(2)}) copy-start(bf16[128,8,128]{2,1,0:T(8,128)(2,1)} %param.14) | copy-start | bytes 786436
  17.8 0.6 copy-start.1
  18.5 1.0 copy-start.6
  19.4 1.1 copy-start.7
  19.7 0.8 copy-start.5
  20.5 0.8 copy-start.4
  21.6 0.8 copy-start.3
  22.5 7.0 %collective-permute-start = (bf16[128,2,128]{2,0,1:T(8,128)(2,1)S(1)}, bf16[128,2,128]{2,0,1:T(8,128)(2,1)S(1)}, u32[]{:S(2)}, u32[]{:S(2)}) collective-permute-start(bf16[128,2,128]{2,0,1:T(8,128)(2,1)S(1)} %get-tuple-element.777), channel_id=1, source_target_pairs={{0,2},{2,4},{4,6},{6,8},{8,10},{10,12},{12,14},{14,0},{1,3},{3,5},... | collective-permute-start | bytes 196616 | tf_op jit(solution)/shard_map/while/body/eval_jaxpr/ppermute | solution.py:9
  29.8 7.0 %collective-permute-start = (bf16[128,2,128]{2,0,1:T(8,128)(2,1)S(1)}, bf16[128,2,128]{2,0,1:T(8,128)(2,1)S(1)}, u32[]{:S(2)}, u32[]{:S(2)}) collective-permute-start(bf16[128,2,128]{2,0,1:T(8,128)(2,1)S(1)} %get-tuple-element.777), channel_id=1, source_target_pairs={{0,2},{2,4},{4,6},{6,8},{8,10},{10,12},{12,14},{14,0},{1,3},{3,5},... | collective-permute-start | bytes 196616 | tf_op jit(solution)/shard_map/while/body/eval_jaxpr/ppermute | solution.py:9
  37.3 7.7 %collective-permute-start = (bf16[128,2,128]{2,0,1:T(8,128)(2,1)S(1)}, bf16[128,2,128]{2,0,1:T(8,128)(2,1)S(1)}, u32[]{:S(2)}, u32[]{:S(2)}) collective-permute-start(bf16[128,2,128]{2,0,1:T(8,128)(2,1)S(1)} %get-tuple-element.777), channel_id=1, source_target_pairs={{0,2},{2,4},{4,6},{6,8},{8,10},{10,12},{12,14},{14,0},{1,3},{3,5},... | collective-permute-start | bytes 196616 | tf_op jit(solution)/shard_map/while/body/eval_jaxpr/ppermute | solution.py:9
  45.4 7.0 %collective-permute-start = (bf16[128,2,128]{2,0,1:T(8,128)(2,1)S(1)}, bf16[128,2,128]{2,0,1:T(8,128)(2,1)S(1)}, u32[]{:S(2)}, u32[]{:S(2)}) collective-permute-start(bf16[128,2,128]{2,0,1:T(8,128)(2,1)S(1)} %get-tuple-element.777), channel_id=1, source_target_pairs={{0,2},{2,4},{4,6},{6,8},{8,10},{10,12},{12,14},{14,0},{1,3},{3,5},... | collective-permute-start | bytes 196616 | tf_op jit(solution)/shard_map/while/body/eval_jaxpr/ppermute | solution.py:9
  52.8 7.0 %collective-permute-start = (bf16[128,2,128]{2,0,1:T(8,128)(2,1)S(1)}, bf16[128,2,128]{2,0,1:T(8,128)(2,1)S(1)}, u32[]{:S(2)}, u32[]{:S(2)}) collective-permute-start(bf16[128,2,128]{2,0,1:T(8,128)(2,1)S(1)} %get-tuple-element.777), channel_id=1, source_target_pairs={{0,2},{2,4},{4,6},{6,8},{8,10},{10,12},{12,14},{14,0},{1,3},{3,5},... | collective-permute-start | bytes 196616 | tf_op jit(solution)/shard_map/while/body/eval_jaxpr/ppermute | solution.py:9
  60.2 7.0 %collective-permute-start = (bf16[128,2,128]{2,0,1:T(8,128)(2,1)S(1)}, bf16[128,2,128]{2,0,1:T(8,128)(2,1)S(1)}, u32[]{:S(2)}, u32[]{:S(2)}) collective-permute-start(bf16[128,2,128]{2,0,1:T(8,128)(2,1)S(1)} %get-tuple-element.777), channel_id=1, source_target_pairs={{0,2},{2,4},{4,6},{6,8},{8,10},{10,12},{12,14},{14,0},{1,3},{3,5},... | collective-permute-start | bytes 196616 | tf_op jit(solution)/shard_map/while/body/eval_jaxpr/ppermute | solution.py:9
  67.6 7.8 %collective-permute-start = (bf16[128,2,128]{2,0,1:T(8,128)(2,1)S(1)}, bf16[128,2,128]{2,0,1:T(8,128)(2,1)S(1)}, u32[]{:S(2)}, u32[]{:S(2)}) collective-permute-start(bf16[128,2,128]{2,0,1:T(8,128)(2,1)S(1)} %get-tuple-element.777), channel_id=1, source_target_pairs={{0,2},{2,4},{4,6},{6,8},{8,10},{10,12},{12,14},{14,0},{1,3},{3,5},... | collective-permute-start | bytes 196616 | tf_op jit(solution)/shard_map/while/body/eval_jaxpr/ppermute | solution.py:9
  76.5 0.8 copy-start.2
  77.4 9.2 %collective-permute-start.1 = (bf16[2,128,2,128]{3,1,2,0:T(8,128)(2,1)S(1)}, bf16[2,128,2,128]{3,1,2,0:T(8,128)(2,1)S(1)}, u32[]{:S(2)}, u32[]{:S(2)}) collective-permute-start(bf16[2,128,2,128]{3,1,2,0:T(8,128)(2,1)S(1)} %get-tuple-element.819), channel_id=1, source_target_pairs={{0,2},{2,4},{4,6},{6,8},{8,10},{10,12},{12,14},{14,0},{1,3},{3,5},... | collective-permute-start | bytes 393224 | tf_op jit(solution)/shard_map/while/body/eval_jaxpr/ppermute | solution.py:9
  77.5 12.3 %collective-permute-start.2 = (f32[2,128,2,128]{3,1,2,0:T(8,128)S(1)}, f32[2,128,2,128]{3,1,2,0:T(8,128)S(1)}, u32[]{:S(2)}, u32[]{:S(2)}) collective-permute-start(f32[2,128,2,128]{3,1,2,0:T(8,128)S(1)} %get-tuple-element.818), channel_id=1, source_target_pairs={{0,2},{2,4},{4,6},{6,8},{8,10},{10,12},{12,14},{14,0},{1,3},{3,5},... | collective-permute-start | bytes 786440 | tf_op jit(solution)/shard_map/while/body/eval_jaxpr/ppermute | solution.py:9
  89.8 8.6 %collective-permute-start.1 = (bf16[2,128,2,128]{3,1,2,0:T(8,128)(2,1)S(1)}, bf16[2,128,2,128]{3,1,2,0:T(8,128)(2,1)S(1)}, u32[]{:S(2)}, u32[]{:S(2)}) collective-permute-start(bf16[2,128,2,128]{3,1,2,0:T(8,128)(2,1)S(1)} %get-tuple-element.819), channel_id=1, source_target_pairs={{0,2},{2,4},{4,6},{6,8},{8,10},{10,12},{12,14},{14,0},{1,3},{3,5},... | collective-permute-start | bytes 393224 | tf_op jit(solution)/shard_map/while/body/eval_jaxpr/ppermute | solution.py:9
  89.9 11.3 %collective-permute-start.2 = (f32[2,128,2,128]{3,1,2,0:T(8,128)S(1)}, f32[2,128,2,128]{3,1,2,0:T(8,128)S(1)}, u32[]{:S(2)}, u32[]{:S(2)}) collective-permute-start(f32[2,128,2,128]{3,1,2,0:T(8,128)S(1)} %get-tuple-element.818), channel_id=1, source_target_pairs={{0,2},{2,4},{4,6},{6,8},{8,10},{10,12},{12,14},{14,0},{1,3},{3,5},... | collective-permute-start | bytes 786440 | tf_op jit(solution)/shard_map/while/body/eval_jaxpr/ppermute | solution.py:9
  101.3 7.7 %collective-permute-start.1 = (bf16[2,128,2,128]{3,1,2,0:T(8,128)(2,1)S(1)}, bf16[2,128,2,128]{3,1,2,0:T(8,128)(2,1)S(1)}, u32[]{:S(2)}, u32[]{:S(2)}) collective-permute-start(bf16[2,128,2,128]{3,1,2,0:T(8,128)(2,1)S(1)} %get-tuple-element.819), channel_id=1, source_target_pairs={{0,2},{2,4},{4,6},{6,8},{8,10},{10,12},{12,14},{14,0},{1,3},{3,5},... | collective-permute-start | bytes 393224 | tf_op jit(solution)/shard_map/while/body/eval_jaxpr/ppermute | solution.py:9
  101.3 10.5 %collective-permute-start.2 = (f32[2,128,2,128]{3,1,2,0:T(8,128)S(1)}, f32[2,128,2,128]{3,1,2,0:T(8,128)S(1)}, u32[]{:S(2)}, u32[]{:S(2)}) collective-permute-start(f32[2,128,2,128]{3,1,2,0:T(8,128)S(1)} %get-tuple-element.818), channel_id=1, source_target_pairs={{0,2},{2,4},{4,6},{6,8},{8,10},{10,12},{12,14},{14,0},{1,3},{3,5},... | collective-permute-start | bytes 786440 | tf_op jit(solution)/shard_map/while/body/eval_jaxpr/ppermute | solution.py:9
  111.8 7.7 %collective-permute-start.1 = (bf16[2,128,2,128]{3,1,2,0:T(8,128)(2,1)S(1)}, bf16[2,128,2,128]{3,1,2,0:T(8,128)(2,1)S(1)}, u32[]{:S(2)}, u32[]{:S(2)}) collective-permute-start(bf16[2,128,2,128]{3,1,2,0:T(8,128)(2,1)S(1)} %get-tuple-element.819), channel_id=1, source_target_pairs={{0,2},{2,4},{4,6},{6,8},{8,10},{10,12},{12,14},{14,0},{1,3},{3,5},... | collective-permute-start | bytes 393224 | tf_op jit(solution)/shard_map/while/body/eval_jaxpr/ppermute | solution.py:9
  111.9 10.6 %collective-permute-start.2 = (f32[2,128,2,128]{3,1,2,0:T(8,128)S(1)}, f32[2,128,2,128]{3,1,2,0:T(8,128)S(1)}, u32[]{:S(2)}, u32[]{:S(2)}) collective-permute-start(f32[2,128,2,128]{3,1,2,0:T(8,128)S(1)} %get-tuple-element.818), channel_id=1, source_target_pairs={{0,2},{2,4},{4,6},{6,8},{8,10},{10,12},{12,14},{14,0},{1,3},{3,5},... | collective-permute-start | bytes 786440 | tf_op jit(solution)/shard_map/while/body/eval_jaxpr/ppermute | solution.py:9
  122.5 7.7 %collective-permute-start.1 = (bf16[2,128,2,128]{3,1,2,0:T(8,128)(2,1)S(1)}, bf16[2,128,2,128]{3,1,2,0:T(8,128)(2,1)S(1)}, u32[]{:S(2)}, u32[]{:S(2)}) collective-permute-start(bf16[2,128,2,128]{3,1,2,0:T(8,128)(2,1)S(1)} %get-tuple-element.819), channel_id=1, source_target_pairs={{0,2},{2,4},{4,6},{6,8},{8,10},{10,12},{12,14},{14,0},{1,3},{3,5},... | collective-permute-start | bytes 393224 | tf_op jit(solution)/shard_map/while/body/eval_jaxpr/ppermute | solution.py:9
  122.6 11.7 %collective-permute-start.2 = (f32[2,128,2,128]{3,1,2,0:T(8,128)S(1)}, f32[2,128,2,128]{3,1,2,0:T(8,128)S(1)}, u32[]{:S(2)}, u32[]{:S(2)}) collective-permute-start(f32[2,128,2,128]{3,1,2,0:T(8,128)S(1)} %get-tuple-element.818), channel_id=1, source_target_pairs={{0,2},{2,4},{4,6},{6,8},{8,10},{10,12},{12,14},{14,0},{1,3},{3,5},... | collective-permute-start | bytes 786440 | tf_op jit(solution)/shard_map/while/body/eval_jaxpr/ppermute | solution.py:9
  134.3 7.7 %collective-permute-start.1 = (bf16[2,128,2,128]{3,1,2,0:T(8,128)(2,1)S(1)}, bf16[2,128,2,128]{3,1,2,0:T(8,128)(2,1)S(1)}, u32[]{:S(2)}, u32[]{:S(2)}) collective-permute-start(bf16[2,128,2,128]{3,1,2,0:T(8,128)(2,1)S(1)} %get-tuple-element.819), channel_id=1, source_target_pairs={{0,2},{2,4},{4,6},{6,8},{8,10},{10,12},{12,14},{14,0},{1,3},{3,5},... | collective-permute-start | bytes 393224 | tf_op jit(solution)/shard_map/while/body/eval_jaxpr/ppermute | solution.py:9
  134.4 12.5 %collective-permute-start.2 = (f32[2,128,2,128]{3,1,2,0:T(8,128)S(1)}, f32[2,128,2,128]{3,1,2,0:T(8,128)S(1)}, u32[]{:S(2)}, u32[]{:S(2)}) collective-permute-start(f32[2,128,2,128]{3,1,2,0:T(8,128)S(1)} %get-tuple-element.818), channel_id=1, source_target_pairs={{0,2},{2,4},{4,6},{6,8},{8,10},{10,12},{12,14},{14,0},{1,3},{3,5},... | collective-permute-start | bytes 786440 | tf_op jit(solution)/shard_map/while/body/eval_jaxpr/ppermute | solution.py:9
  147.0 7.7 %collective-permute-start.1 = (bf16[2,128,2,128]{3,1,2,0:T(8,128)(2,1)S(1)}, bf16[2,128,2,128]{3,1,2,0:T(8,128)(2,1)S(1)}, u32[]{:S(2)}, u32[]{:S(2)}) collective-permute-start(bf16[2,128,2,128]{3,1,2,0:T(8,128)(2,1)S(1)} %get-tuple-element.819), channel_id=1, source_target_pairs={{0,2},{2,4},{4,6},{6,8},{8,10},{10,12},{12,14},{14,0},{1,3},{3,5},... | collective-permute-start | bytes 393224 | tf_op jit(solution)/shard_map/while/body/eval_jaxpr/ppermute | solution.py:9
  147.1 10.5 %collective-permute-start.2 = (f32[2,128,2,128]{3,1,2,0:T(8,128)S(1)}, f32[2,128,2,128]{3,1,2,0:T(8,128)S(1)}, u32[]{:S(2)}, u32[]{:S(2)}) collective-permute-start(f32[2,128,2,128]{3,1,2,0:T(8,128)S(1)} %get-tuple-element.818), channel_id=1, source_target_pairs={{0,2},{2,4},{4,6},{6,8},{8,10},{10,12},{12,14},{14,0},{1,3},{3,5},... | collective-permute-start | bytes 786440 | tf_op jit(solution)/shard_map/while/body/eval_jaxpr/ppermute | solution.py:9
  157.8 9.1 %collective-permute-start.3 = (f32[2,128,2,128]{3,2,1,0:T(2,128)S(1)}, f32[2,128,2,128]{3,2,1,0:T(2,128)S(1)}, u32[]{:S(2)}, u32[]{:S(2)}) collective-permute-start(f32[2,128,2,128]{3,2,1,0:T(2,128)S(1)} %copy.46), channel_id=1, source_target_pairs={{0,2},{2,4},{4,6},{6,8},{8,10},{10,12},{12,14},{14,0},{1,3},{3,5},... | collective-permute-start | bytes 786440 | tf_op jit(solution)/shard_map/ppermute | solution.py:9
where the time goes:
time: 168 us
  waiting for transfers between devices  107 us (64%)
  local copies, waits for them, and re-layouts  17.7 us (11%)
  blocking collectives  13.1 us (8%)
  matrix products  11.7 us (7%)
  loops' own time  10.4 us (6%)
  starting transfers between devices  2.75 us (2%)
  other arithmetic  2.71 us (2%)
  between operations  2.19 us (1%)
    ppermute x22, waiting for transfers between devices, passed_along(): lax.ppermute(value, axis, [(i, (i + by) % peers) for i in range(peers)])  107 us
    unnamed x1, blocking collectives  13.1 us
    dynamic_slice x15, local copies, waits for them, and re-layouts, masked_scores(): key_positions = block_starts[source_block] * tok_rows + row_index  8.86 us
    unnamed x24, local copies, waits for them, and re-layouts  5.71 us
    another operation x1, loops' own time, on_device(): lax.fori_loop(1, cycle_size, back_loop, (query_grad, grad_pair, travelling))  5.4 us
    another operation x1, loops' own time, on_device(): lax.fori_loop(1, cycle_size, stats_loop, (running, key_vectors))  4.98 us
    dot_general x15, matrix products, masked_scores(): jnp.einsum('ighd,jgd->ghij', grouped_query, key_block, preferred_element_...  3.92 us
  transfers between devices with their start and end apart: 22, of which 22 were waited for; matrix products, arithmetic and copies ran while one was open for 12% of the time, Pallas kernels for 0%

commit v1 on v0

v1 whole, which is shorter than its diff:
```python
import functools

import jax
import jax.numpy as jnp
from jax import lax
from jax.experimental import pallas as pl
from jax.experimental.pallas import tpu as pltpu
from jax.sharding import PartitionSpec as P

MESH = pl.DeviceIdType.MESH
LOG2E = 1.4426950408889634
F32 = jnp.float32
BF16 = jnp.bfloat16


def dot_nt(a, b):
    return lax.dot_general(a, b, (((1,), (1,)), ((), ())), preferred_element_type=F32)


def dot_nn(a, b):
    return lax.dot_general(a, b, (((1,), (0,)), ((), ())), preferred_element_type=F32)


def kernel(Z, Y, G, H, T, D, *refs):
    (q_ref, k_ref, v_ref, fo_ref, do_ref, off_ref, dq_ref, dk_ref, dv_ref,
     tmp, qs, dos, kbuf, vbuf, kt, s_scr, delta, dqt,
     partv, partk, ysv, ysk, yrv, yrk, zsv, zsk, zrv, zrk,
     kz_s, kz_r, ky_s, ky_r, vz_s, vz_r, vy_s, vy_r,
     gvy_s, gvy_r, gky_s, gky_r, gvz_s, gvz_r, gkz_s, gkz_r) = refs
    me = lax.axis_index("ctx")
    z, y = me // Y, me % Y
    scale = D ** (-0.5)
    N = Z * Y
    R = G * T
    Q = H * T

    def at(zz, yy):
        return {"ctx": zz * Y + yy}

    def up(d):
        return lax.rem(z + d, Z)

    def down(d):
        return lax.rem(z + Z - d, Z)

    other = 1 - y

    barrier = pltpu.get_barrier_semaphore()
    for d in range(1, Z):
        pl.semaphore_signal(barrier, inc=1, device_id=at(up(d), y), device_id_type=MESH)
    if Y == 2:
        pl.semaphore_signal(barrier, inc=1, device_id=at(z, other), device_id_type=MESH)

    def split_heads(src, heads, put):
        tmp[0:T * heads, :] = src[...].astype(F32)
        for h in range(heads):
            put(h, tmp[pl.ds(h, T, stride=heads), :])

    def put_k(g, x):
        kbuf[me, pl.ds(g * T, T), :] = x.astype(BF16)

    def put_v(g, x):
        vbuf[me, pl.ds(g * T, T), :] = x.astype(BF16)

    own_off = off_ref[0].astype(F32)
    split_heads(k_ref, G, put_k)
    kbuf[me, pl.ds(R, 16), :] = jnp.full((16, D), own_off, F32).astype(BF16)
    split_heads(v_ref, G, put_v)
    pl.semaphore_wait(barrier, Z - 1 + (1 if Y == 2 else 0))

    def zcopy(buf, d, ss, rs, block):
        return pltpu.make_async_remote_copy(
            src_ref=buf.at[block], dst_ref=buf.at[block], send_sem=ss.at[d], recv_sem=rs.at[d],
            device_id=at(up(d), y), device_id_type=MESH)

    def ycopy(buf, d, ss, rs, block):
        return pltpu.make_async_remote_copy(
            src_ref=buf.at[block], dst_ref=buf.at[block], send_sem=ss.at[d], recv_sem=rs.at[d],
            device_id=at(z, other), device_id_type=MESH)

    def start_own(buf, zs, zr, ys, yr):
        if Y == 2:
            ycopy(buf, 0, ys, yr, me).start()
        for d in range(1, Z):
            zcopy(buf, d, zs, zr, me).start()

    def forward(buf, d, zs, zr, ys, yr):
        block = down(d) * Y + y
        zcopy(buf, d, zs, zr, block).wait_recv()
        if Y == 2:
            ycopy(buf, d, ys, yr, block).start()

    def arrive_y(buf, d, ys, yr):
        if Y == 2:
            ycopy(buf, d, ys, yr, down(d) * Y + other).wait_recv()

    start_own(kbuf, kz_s, kz_r, ky_s, ky_r)

    def put_q(h, x):
        qs[h // H, pl.ds((h % H) * T, T), :] = x.astype(BF16)

    split_heads(q_ref, G * H, put_q)

    def put_do(h, x):
        dos[h // H, pl.ds((h % H) * T, T), :] = x.astype(BF16)

    split_heads(do_ref, G * H, put_do)
    tmp[...] = do_ref[...].astype(F32) * fo_ref[...].astype(F32)
    for h in range(G * H):
        prod = tmp[pl.ds(h, T, stride=G * H), :]
        delta[h // H, :, pl.ds((h % H) * T, T)] = jnp.sum(prod.T, axis=0, keepdims=True)

    for d in range(1, Z):
        forward(kbuf, d, kz_s, kz_r, ky_s, ky_r)
    start_own(vbuf, vz_s, vz_r, vy_s, vy_r)
    for d in range(Z):
        arrive_y(kbuf, d, ky_s, ky_r)

    C = Y * T

    def key_rows(buf, c, g):
        return jnp.concatenate([buf[c * Y + i, pl.ds(g * T, T), :] for i in range(Y)], axis=0)

    lead = (lax.broadcasted_iota(jnp.int32, (T, Q), 0)
            - lax.broadcasted_iota(jnp.int32, (T, Q), 1) % T).astype(F32)

    def score_step(c, tops):
        new = []
        for g in range(G):
            s = dot_nt(key_rows(kbuf, c, g), qs[g]) * (scale * LOG2E)
            parts = []
            for i in range(Y):
                off = kbuf[c * Y + i, pl.ds(R, 16), :][0:1, :].astype(F32)
                gap = (own_off - off) * T
                gap = jnp.concatenate([gap] * (Q // D), axis=1)
                parts.append(jnp.where(lead <= gap, s[i * T:(i + 1) * T], -1e30))
            s = jnp.concatenate(parts, axis=0)
            s_scr[g, pl.ds(c * C, C), :] = s
            top = tops[g]
            top = jnp.maximum(top, jnp.max(s.reshape(C // 8, 8, Q), axis=0))
            new.append(top)
        return tuple(new)

    tops = lax.fori_loop(0, Z, score_step, tuple(jnp.full((8, Q), -1e30, F32) for _ in range(G)))
    tops = [jnp.max(t, axis=0, keepdims=True) for t in tops]
    if Z > 1:
        forward(vbuf, 1, vz_s, vz_r, vy_s, vy_r)

    def total_step(c, sums):
        new = []
        for g in range(G):
            e = jnp.exp2(s_scr[g, pl.ds(c * C, C), :] - tops[g])
            s_scr[g, pl.ds(c * C, C), :] = e
            new.append(sums[g] + jnp.sum(e.reshape(C // 8, 8, Q), axis=0))
        return tuple(new)

    sums = lax.fori_loop(0, Z, total_step, tuple(jnp.zeros((8, Q), F32) for _ in range(G)))
    inv = [1.0 / jnp.sum(t, axis=0, keepdims=True) for t in sums]
    for d in range(2, Z):
        forward(vbuf, d, vz_s, vz_r, vy_s, vy_r)

    def gycopy(ysend, yrecv, c, ss, rs):
        return pltpu.make_async_remote_copy(
            src_ref=ysend.at[c], dst_ref=yrecv.at[c], send_sem=ss.at[c], recv_sem=rs.at[c],
            device_id=at(z, other), device_id_type=MESH)

    def gzcopy(zsend, zrecv, d, ss, rs):
        return pltpu.make_async_remote_copy(
            src_ref=zsend.at[d], dst_ref=zrecv.at[d], send_sem=ss.at[d], recv_sem=rs.at[d],
            device_id=at(up(d), y), device_id_type=MESH)

    def keep_partial(x_buf, part, ysend, c, g):
        if Y == 2:
            part[c, pl.ds(g * T, T), :] = x_buf[pl.ds(y * T, T), :]
            ysend[c, pl.ds(g * T, T), :] = x_buf[pl.ds(other * T, T), :].astype(BF16)
        else:
            part[c, pl.ds(g * T, T), :] = x_buf[...]

    def value_step(i, carry):
        c = lax.rem(z + 1 + i, Z)
        for g in range(G):
            p = s_scr[g, pl.ds(c * C, C), :] * inv[g]
            s_scr[g, pl.ds(c * C, C), :] = p
            dqt[0:C, 0:D] = dot_nn(p.astype(BF16), dos[g])
            keep_partial(dqt.at[0:C, 0:D], partv, ysv, c, g)
        if Y == 2:
            gycopy(ysv, yrv, c, gvy_s, gvy_r).start()
        return carry

    lax.fori_loop(0, Z, value_step, 0)

    for d in range(Z):
        arrive_y(vbuf, d, vy_s, vy_r)

    def send_z(part, ysend, yrecv, zsend, zrecv, d, ys, yr, zs, zr):
        c = up(d)
        total = part[c]
        if Y == 2:
            gycopy(ysend, yrecv, c, ys, yr).wait_recv()
            total = total + yrecv[c].astype(F32)
        zsend[d] = total.astype(BF16)
        gzcopy(zsend, zrecv, d, zs, zr).start()

    for g in range(G):
        dqt[pl.ds(g * D, D), :] = jnp.zeros((D, Q), F32)
        kt[...] = jnp.zeros_like(kt)

    def key_chunk(c):
        for g in range(G):
            kc = key_rows(kbuf, c, g)
            dp = dot_nt(key_rows(vbuf, c, g), dos[g])
            ds = (s_scr[g, pl.ds(c * C, C), :] * (dp - delta[g])).astype(BF16)
            kt[...] = dot_nn(ds, qs[g]) * scale
            keep_partial(kt, partk, ysk, c, g)
            dqt[pl.ds(g * D, D), :] += dot_nn(kc.astype(F32).T.astype(BF16), ds)
        if Y == 2:
            gycopy(ysk, yrk, c, gky_s, gky_r).start()

    def key_step(i, carry):
        key_chunk(lax.rem(z + 1 + i, Z))
        send_z(partv, ysv, yrv, zsv, zrv, i + 1, gvy_s, gvy_r, gvz_s, gvz_r)
        return carry

    lax.fori_loop(0, Z - 1, key_step, 0)
    key_chunk(z)

    def send_k(i, carry):
        send_z(partk, ysk, yrk, zsk, zrk, i + 1, gky_s, gky_r, gkz_s, gkz_r)
        return carry

    lax.fori_loop(0, Z - 1, send_k, 0)

    for g in range(G):
        for h in range(H):
            dq_ref[pl.ds(g * H + h, T, stride=G * H), :] = (
                dqt[pl.ds(g * D, D), pl.ds(h * T, T)].T * scale)

    def finish(out, part, ysend, yrecv, zsend, zrecv, ys, yr, zs, zr):
        total = part[z]
        if Y == 2:
            gycopy(ysend, yrecv, z, ys, yr).wait_recv()
            total = total + yrecv[z].astype(F32)

        def add(d, acc):
            gzcopy(zsend, zrecv, d, zs, zr).wait_recv()
            return acc + zrecv[d].astype(F32)

        part[z] = lax.fori_loop(1, Z, add, total)
        for g in range(G):
            out[pl.ds(g, T, stride=G), :] = part[z, pl.ds(g * T, T), :]

    finish(dv_ref, partv, ysv, yrv, zsv, zrv, gvy_s, gvy_r, gvz_s, gvz_r)
    finish(dk_ref, partk, ysk, yrk, zsk, zrk, gky_s, gky_r, gkz_s, gkz_r)

    for d in range(Z):
        block = down(d) * Y + y
        if d > 0:
            zcopy(kbuf, d, kz_s, kz_r, me).wait_send()
            zcopy(vbuf, d, vz_s, vz_r, me).wait_send()
            gzcopy(zsv, zrv, d, gvz_s, gvz_r).wait_send()
            gzcopy(zsk, zrk, d, gkz_s, gkz_r).wait_send()
        if Y == 2:
            ycopy(kbuf, d, ky_s, ky_r, block).wait_send()
            ycopy(vbuf, d, vy_s, vy_r, block).wait_send()
            gycopy(ysv, yrv, d, gvy_s, gvy_r).wait_send()
            gycopy(ysk, yrk, d, gky_s, gky_r).wait_send()


def on_device(Y, query_vectors, key_vectors, value_rows, forward_out, out_grad, block_offsets):
    T, QH, D = query_vectors.shape
    G = key_vectors.shape[1]
    H = QH // G
    N = lax.axis_size("ctx")
    Z = N // Y
    R, Q, C = G * T, H * T, Y * T
    vmem = pl.BlockSpec(memory_space=pltpu.VMEM)
    smem = pl.BlockSpec(memory_space=pltpu.SMEM)
    blocks = lambda dt: pltpu.VMEM((Z, R, D), dt)
    dq, dk, dv = pl.pallas_call(
        functools.partial(kernel, Z, Y, G, H, T, D),
        out_shape=(
            jax.ShapeDtypeStruct((T * QH, D), F32),
            jax.ShapeDtypeStruct((R, D), F32),
            jax.ShapeDtypeStruct((R, D), F32),
        ),
        in_specs=[vmem] * 5 + [smem],
        out_specs=[vmem] * 3,
        scratch_shapes=[
            pltpu.VMEM((T * QH, D), F32),
            pltpu.VMEM((G, Q, D), BF16),
            pltpu.VMEM((G, Q, D), BF16),
            pltpu.VMEM((N, R + 16, D), BF16),
            pltpu.VMEM((N, R, D), BF16),
            pltpu.VMEM((C, D), F32),
            pltpu.VMEM((G, N * T, Q), F32),
            pltpu.VMEM((G, 1, Q), F32),
            pltpu.VMEM((G * D, Q), F32),
            blocks(F32), blocks(F32),
            blocks(BF16), blocks(BF16), blocks(BF16), blocks(BF16),
            blocks(BF16), blocks(BF16), blocks(BF16), blocks(BF16),
        ] + [pltpu.SemaphoreType.DMA((Z,))] * 16,
        compiler_params=pltpu.CompilerParams(
            collective_id=0, has_side_effects=True, vmem_limit_bytes=48 * 1024 * 1024
        ),
        cost_estimate=pl.CostEstimate(
            flops=10 * G * Q * N * T * D, bytes_accessed=4 * T * QH * D * 4,
            transcendentals=G * Q * N * T,
        ),
    )(
        query_vectors.reshape(T * QH, D), key_vectors.reshape(R, D), value_rows.reshape(R, D),
        forward_out.reshape(T * QH, D), out_grad.reshape(T * QH, D), block_offsets,
    )
    return dq.reshape(T, QH, D), dk.reshape(T, G, D), dv.reshape(T, G, D)


def solution(mesh):
    pair = 2 if mesh.shape["groups"] == 2 and mesh.shape["ctx"] % 2 == 0 else 1
    tokens = P(("groups", "ctx"), "heads", None)
    return jax.shard_map(
        functools.partial(on_device, pair), mesh=mesh,
        in_specs=(tokens,) * 5 + (P(("groups", "ctx")),),
        out_specs=(tokens,) * 3, check_vma=False,
    )
```

time: 168 us -> 47.1 us (0.28)
  waiting for transfers between devices: 107 us -> 0 us
  Pallas kernels: 0 us -> 38.9 us
  blocking collectives: 13.1 us -> 0 us
  matrix products: 11.7 us -> 0 us
  local copies, waits for them, and re-layouts: 17.7 us -> 6.63 us
  loops' own time: 10.4 us -> 0 us
  starting transfers between devices: 2.75 us -> 0 us
  other arithmetic: 2.71 us -> 0 us
    ppermute x22 -> x0, waiting for transfers between devices: 107 us -> none  [passed_along(): lax.ppermute(value, axis, [(i, (i + by) % peers) for i in range(peers)])]
    pallas_call x0 -> x1, Pallas kernels: none -> 38.9 us  [on_device(): pl.pallas_call(functools.partial(kernel, Z, Y, G, H, T, D), out_shape=(ja...]
    unnamed x1 -> x0, blocking collectives: 13.1 us -> none
    dot_general x47 -> x0, matrix products: 11.7 us -> none  [the longest x15 3.92 us: masked_scores(): jnp.einsum('ighd,jgd->ghij', grouped_query, key_block, preferred_element_...]
    another operation x2 -> x0, loops' own time: 10.4 us -> none  [the longest x1 5.4 us: on_device(): lax.fori_loop(1, cycle_size, back_loop, (query_grad, grad_pair, travelling))]
    dynamic_slice x15 -> x0, local copies, waits for them, and re-layouts: 8.86 us -> none  [masked_scores(): key_positions = block_starts[source_block] * tok_rows + row_index]
    ppermute x22 -> x0, starting transfers between devices: 2.75 us -> none  [passed_along(): lax.ppermute(value, axis, [(i, (i + by) % peers) for i in range(peers)])]
    unnamed x24 -> x13, local copies, waits for them, and re-layouts: 5.71 us -> 6.63 us
  transfers between devices with their start and end apart: 22 -> 0, of which waited for: 22 -> 0; matrix products, arithmetic and copies ran while one was open for 12% -> 0% of each run, Pallas kernels for 0% -> 0%
where the time goes in v1:
time: 47.1 us; the launch traced here: 46.8 us
  Pallas kernels  38.9 us (83%)
  local copies, waits for them, and re-layouts  6.63 us (14%)
  between operations  1.3 us (3%)
    pallas_call x1, Pallas kernels, on_device(): pl.pallas_call(functools.partial(kernel, Z, Y, G, H, T, D), out_shape=(ja...  38.9 us
    unnamed x13, local copies, waits for them, and re-layouts  6.63 us

profile of v1, /device:TPU:0, one launch (start us, length us, event | category | flops | bytes accessed | tf_op | source)
XLA Modules:
  0.0 46.8 jit_solution(2556517672441587567)
XLA Ops:
  1.3 0.0 copy-start
  1.3 0.9 %copy-done = bf16[128,8,128]{2,1,0:T(8,128)(2,1)S(1)} copy-done((bf16[128,8,128]{2,1,0:T(8,128)(2,1)S(1)}, bf16[128,8,128]{2,1,0:T(8,128)(2,1)}, u32[]{:S(2)}) %copy-start) | copy-done | bytes 262168
  2.2 0.0 copy-start.1
  2.2 0.9 %copy-done.1 = bf16[128,8,128]{2,1,0:T(8,128)(2,1)S(1)} copy-done((bf16[128,8,128]{2,1,0:T(8,128)(2,1)S(1)}, bf16[128,8,128]{2,1,0:T(8,128)(2,1)}, u32[]{:S(2)}) %copy-start.1) | copy-done | bytes 262168
  3.2 0.0 copy-start.2
  3.2 0.9 %copy-done.2 = bf16[128,8,128]{2,1,0:T(8,128)(2,1)S(1)} copy-done((bf16[128,8,128]{2,1,0:T(8,128)(2,1)S(1)}, bf16[128,8,128]{2,1,0:T(8,128)(2,1)}, u32[]{:S(2)}) %copy-start.2) | copy-done | bytes 262168
  4.1 0.0 copy-start.3
  4.1 0.8 %copy-done.3 = bf16[128,2,128]{2,1,0:T(2,128)(2,1)S(1)} copy-done((bf16[128,2,128]{2,1,0:T(2,128)(2,1)S(1)}, bf16[128,2,128]{2,1,0:T(2,128)(2,1)}, u32[]{:S(2)}) %copy-start.3) | copy-done | bytes 65560
  5.0 0.0 copy-start.4
  5.0 0.8 %copy-done.4 = bf16[128,2,128]{2,1,0:T(2,128)(2,1)S(1)} copy-done((bf16[128,2,128]{2,1,0:T(2,128)(2,1)S(1)}, bf16[128,2,128]{2,1,0:T(2,128)(2,1)}, u32[]{:S(2)}) %copy-start.4) | copy-done | bytes 65560
  5.8 38.9 %shard_map.85 = (f32[1024,128]{1,0:T(8,128)S(1)}, f32[256,128]{1,0:T(8,128)S(1)}, f32[256,128]{1,0:T(8,128)S(1)}) custom-call(bf16[1024,128]{1,0:T(8,128)(2,1)S(1)} %bitcast.11, bf16[256,128]{1,0:T(8,128)(2,1)S(1)} %bitcast.14, bf16[256,128]{1,0:T(8,128)(2,1)S(1)} %bitcast.15, bf16[1024,128]{1,0:T(8,128)(2,1)S(1)} %bitcast.12, ...), custom_call_target="tpu_custom_call" | custom-call | flops 1342177280 | bytes 2097152 | tf_op jit(solution)/shard_map/pallas_call | solution.py:279
  44.7 0.8 %copy.13 = f32[128,8,128]{2,1,0:T(8,128)} copy(f32[128,8,128]{2,1,0:T(8,128)S(1)} %bitcast.8) | data formatting | bytes 1048576
  45.5 0.7 %copy.14 = f32[128,2,128]{2,1,0:T(2,128)} copy(f32[128,2,128]{2,1,0:T(2,128)S(1)} %bitcast.10) | data formatting | bytes 262144
  46.1 0.7 %copy.15 = f32[128,2,128]{2,1,0:T(2,128)} copy(f32[128,2,128]{2,1,0:T(2,128)S(1)} %bitcast.9) | data formatting | bytes 262144
Async XLA Ops:
  1.3 1.0 %copy-start = (bf16[128,8,128]{2,1,0:T(8,128)(2,1)S(1)}, bf16[128,8,128]{2,1,0:T(8,128)(2,1)}, u32[]{:S(2)}) copy-start(bf16[128,8,128]{2,1,0:T(8,128)(2,1)} %param.6) | copy-start | bytes 786436
  2.2 0.9 %copy-start.1 = (bf16[128,8,128]{2,1,0:T(8,128)(2,1)S(1)}, bf16[128,8,128]{2,1,0:T(8,128)(2,1)}, u32[]{:S(2)}) copy-start(bf16[128,8,128]{2,1,0:T(8,128)(2,1)} %param.9) | copy-start | bytes 786436
  3.2 0.9 %copy-start.2 = (bf16[128,8,128]{2,1,0:T(8,128)(2,1)S(1)}, bf16[128,8,128]{2,1,0:T(8,128)(2,1)}, u32[]{:S(2)}) copy-start(bf16[128,8,128]{2,1,0:T(8,128)(2,1)} %param.10) | copy-start | bytes 786436
  4.1 0.8 %copy-start.3 = (bf16[128,2,128]{2,1,0:T(2,128)(2,1)S(1)}, bf16[128,2,128]{2,1,0:T(2,128)(2,1)}, u32[]{:S(2)}) copy-start(bf16[128,2,128]{2,1,0:T(2,128)(2,1)} %param.7) | copy-start | bytes 196612
  5.0 0.8 %copy-start.4 = (bf16[128,2,128]{2,1,0:T(2,128)(2,1)S(1)}, bf16[128,2,128]{2,1,0:T(2,128)(2,1)}, u32[]{:S(2)}) copy-start(bf16[128,2,128]{2,1,0:T(2,128)(2,1)} %param.8) | copy-start | bytes 196612
